TPU v7x, 512 devices: a whole 4x4x16 slice. The times are simulated.
512 devices in a mesh: space: 64 (over y, z), dp: 8 (over x, core).
Axes of the slice: x: 4, y: 4, z: 16, core: 2. Of those that a mesh axis runs over, the one named last changes fastest.
Arguments:
- coarse_latents: bfloat16 [8, 4096, 512], P('dp', 'space'), may hold values from -6 to 6
- active_blocks: int32 [8, 128], P('dp'), may hold values from 0 to 4095, as said below
- face_links: int32 [8, 128, 6], P('dp', 'space'), may hold values from -1 to 127, as said below
- cotangent: bfloat16 [8, 128, 8, 8, 256], P('dp', 'space'), may hold values from -6 to 6
- up_weight: bfloat16 [64, 2048], replicated, may hold values from -0.75 to 0.75
- conv_one: bfloat16 [27, 32, 32], replicated, may hold values from -0.21875 to 0.21875
- conv_two: bfloat16 [27, 32, 32], replicated, may hold values from -0.21875 to 0.21875
Outputs:
- fine: bfloat16 [8, 128, 8, 8, 256], P('dp', 'space')
- grad_one: float32 [27, 32, 32], replicated
- grad_two: float32 [27, 32, 32], replicated
Inputs may be any that keep to these rules, and one draw needn't show every extreme that they name: `active_blocks`: call the bricks at positions i * 2 to (i + 1) * 2 - 1 group i and the block rows i * 64 to (i + 1) * 64 - 1 range i. At most 2 bricks of one group take their blocks from one range, and in every scene every group has exactly 2 from some range. `face_links`: links are mutual: if brick h is the neighbour of g across face f, g is the neighbour of h across the opposite face. A neighbour of brick g lies at a position whose quotient by 2 differs from that of g by at most one; across a -x, -y or -z face that quotient is never larger than that of g, across a +x, +y or +z face never smaller.
All inputs are finite; a program needn't handle non-finite values.
Results may differ from a plain program's by a relative error of at most 0.0057.
Values may be sent and summed in bfloat16 or wider, within the bound.
A program may use at most 128 MiB of HBM per device.

v0:
```python
import math

import jax
import jax.numpy as jnp
from jax import lax
from jax.sharding import PartitionSpec as P


def passed_along(value, axis, steps):
    count = lax.axis_size(axis)
    first, last = (max(0, -steps), min(count, count - steps))
    return lax.ppermute(value, axis, [(source, source + steps) for source in range(first, last)])


def depth_select(extent):
    inputs_z = jnp.arange(extent + 2)[None, :, None]
    outputs_z = jnp.arange(extent)[None, None, :]
    offsets_z = jnp.arange(3)[:, None, None]
    return (inputs_z == outputs_z + offsets_z).astype(jnp.float32)


def band_matrix(weights, extent):
    channels = weights.shape[1]
    cube = weights.astype(jnp.float32).reshape(3, 3, 3, channels, channels)
    banded = jnp.einsum(
        "dpq,abdio->abpiqo", depth_select(extent), cube, precision=lax.Precision.HIGHEST
    )
    return banded.reshape(3, 3, (extent + 2) * channels, extent * channels).astype(jnp.bfloat16)


def apply_band(padded, banded, extent):
    total = None
    for shift_x in range(3):
        for shift_y in range(3):
            window = padded[:, shift_x : shift_x + extent, shift_y : shift_y + extent, :]
            term = jnp.einsum(
                "nxyp,pq->nxyq",
                window,
                banded[shift_x, shift_y],
                preferred_element_type=jnp.float32,
            )
            total = term if total is None else total + term
    return total


def band_gradient(padded, gradient, extent, channels):
    select = depth_select(extent)
    pieces = []
    for shift_x in range(3):
        for shift_y in range(3):
            window = padded[:, shift_x : shift_x + extent, shift_y : shift_y + extent, :]
            outer = jnp.einsum(
                "nxyp,nxyq->pq", window, gradient, preferred_element_type=jnp.float32
            )
            outer = outer.reshape(extent + 2, channels, extent, channels)
            pieces.append(
                jnp.einsum("dpq,piqo->dio", select, outer, precision=lax.Precision.HIGHEST)
            )
    return jnp.stack(pieces).reshape(27, channels, channels)


def lift_bricks(latent_rows, up_weight, extent, channels):
    bricks_here = latent_rows.shape[0]
    blocks = latent_rows.reshape(bricks_here, 8, -1)
    cells = jnp.einsum("nci,io->nco", blocks, up_weight, preferred_element_type=jnp.float32)
    half = extent // 2
    shaped = cells.reshape(bricks_here, 2, 2, 2, half, half, half, channels)
    shaped = shaped.transpose(0, 1, 4, 2, 5, 3, 6, 7)
    return shaped.reshape(bricks_here, extent, extent, extent * channels).astype(jnp.bfloat16)


def face_planes(volume, channels):
    bricks_here, extent = (volume.shape[0], volume.shape[1])
    planes = [
        volume[:, 0],
        volume[:, extent - 1],
        volume[:, :, 0],
        volume[:, :, extent - 1],
        volume[:, :, :, 0:channels],
        volume[:, :, :, (extent - 1) * channels :],
    ]
    return jnp.stack([one_plane.reshape(bricks_here, -1) for one_plane in planes], axis=1)


def share_faces(stacked):
    from_left = passed_along(stacked, "space", 1)
    from_right = passed_along(stacked, "space", -1)
    return jnp.stack([from_left, stacked, from_right], axis=1)


def fill_padding(volume, face_pool, face_links, position, channels):
    bricks_here, extent = (volume.shape[0], volume.shape[1])
    neighbour = jnp.maximum(face_links, 0)
    source = jnp.clip(neighbour // bricks_here - position + 1, 0, 2)
    face_index = jnp.arange(6, dtype=jnp.int32)[None, :]
    row_index = (source * bricks_here + neighbour % bricks_here) * 6 + (face_index ^ 1)
    flattened = face_pool.reshape(3 * bricks_here * 6, -1)
    picked = jnp.take(flattened, row_index.reshape(-1), axis=0).reshape(bricks_here, 6, -1)
    picked = jnp.where((face_links >= 0)[:, :, None], picked, jnp.zeros((), picked.dtype))
    padded = jnp.pad(volume, ((0, 0), (1, 1), (1, 1), (channels, channels)))
    inside_range = slice(1, extent + 1)
    middle_range = slice(channels, (extent + 1) * channels)
    flat_face = (bricks_here, extent, extent * channels)
    depth_face = (bricks_here, extent, extent, channels)
    padded = padded.at[:, 0, inside_range, middle_range].set(picked[:, 0].reshape(flat_face))
    padded = padded.at[:, extent + 1, inside_range, middle_range].set(
        picked[:, 1].reshape(flat_face)
    )
    padded = padded.at[:, inside_range, 0, middle_range].set(picked[:, 2].reshape(flat_face))
    padded = padded.at[:, inside_range, extent + 1, middle_range].set(
        picked[:, 3].reshape(flat_face)
    )
    padded = padded.at[:, inside_range, inside_range, 0:channels].set(
        picked[:, 4].reshape(depth_face)
    )
    padded = padded.at[:, inside_range, inside_range, (extent + 1) * channels :].set(
        picked[:, 5].reshape(depth_face)
    )
    return padded


def body(coarse_latents, active_blocks, face_links, cotangent, up_weight, conv_one, conv_two):
    position = lax.axis_index("space")
    devices = lax.axis_size("space")
    bricks_here = face_links.shape[1]
    extent = cotangent.shape[2]
    channels = conv_one.shape[1]
    blocks_here = coarse_latents.shape[1]
    local_rows = coarse_latents[0]
    listed = active_blocks[0]
    mine = lax.dynamic_slice_in_dim(listed, position * bricks_here, bricks_here)
    owners = mine // blocks_here
    wanted = listed.reshape(devices, bricks_here)
    held = wanted // blocks_here == position
    local_index = jnp.clip(wanted - position * blocks_here, 0, blocks_here - 1)
    packed = jnp.where(
        held[:, :, None], jnp.take(local_rows, local_index, axis=0), jnp.zeros((), local_rows.dtype)
    )
    received = lax.all_to_all(packed, "space", split_axis=0, concat_axis=0, tiled=True)
    latent_rows = received[owners, jnp.arange(bricks_here)]
    lifted = lift_bricks(latent_rows, up_weight, extent, channels)
    links = face_links[0]
    upstream = cotangent[0]
    lifted_pool = share_faces(face_planes(lifted, channels)[None])[0]
    lifted_pad = fill_padding(lifted, lifted_pool, links, position, channels)
    band_one = band_matrix(conv_one, extent)
    band_two = band_matrix(conv_two, extent)
    band_back = band_matrix(jnp.flip(conv_two, axis=0).transpose(0, 2, 1), extent)
    pre = apply_band(lifted_pad, band_one, extent)
    hidden = jax.nn.silu(pre).astype(jnp.bfloat16)
    hidden_pool = share_faces(face_planes(hidden, channels)[None])[0]
    hidden_pad = fill_padding(hidden, hidden_pool, links, position, channels)
    fine = (lifted.astype(jnp.float32) + apply_band(hidden_pad, band_two, extent)).astype(
        jnp.bfloat16
    )
    scale = 1.0 / math.sqrt(lax.axis_size("dp") * devices * bricks_here * extent**3)
    second_local = band_gradient(hidden_pad, upstream, extent, channels) * scale
    upstream_pool = share_faces(face_planes(upstream, channels)[None])[0]
    upstream_pad = fill_padding(upstream, upstream_pool, links, position, channels)
    back = apply_band(upstream_pad, band_back, extent)
    sigmoid = jax.nn.sigmoid(pre)
    grad_pre = (back * sigmoid * (1.0 + pre * (1.0 - sigmoid))).astype(jnp.bfloat16)
    first_local = band_gradient(lifted_pad, grad_pre, extent, channels) * scale
    grad_one, grad_two = lax.psum((first_local, second_local), ("space", "dp"))
    return (fine[None], grad_one, grad_two)


def solution(mesh):
    return jax.shard_map(
        body,
        mesh=mesh,
        in_specs=(
            P("dp", "space", None),
            P("dp", None),
            P("dp", "space", None),
            P("dp", "space", None, None, None),
            P(),
            P(),
            P(),
        ),
        out_specs=(P("dp", "space", None, None, None), P(), P()),
        check_vma=False,
    )
```

profile of v0, /device:TPU:1, one launch (start us, length us, event | category | flops | bytes accessed | tf_op | source)
XLA Modules:
  0.0 757.4 jit_solution(1332796535409045901)
XLA Ops:
  13.7 5.0 collective-permute-start.4
  25.9 19.5 %all-to-all-start = ((bf16[64,2,512]{2,1,0:T(2,128)(2,1)}), bf16[64,2,512]{2,1,0:T(2,128)(2,1)S(1)}, u32[]{:S(2)}, u32[]{:S(2)}) async-start(bf16[64,2,512]{2,1,0:T(2,128)(2,1)} %broadcast_select_fusion.1), calls=%async_computation | async-start | bytes 262144 | tf_op jit(solution)/shard_map/all_to_all | solution.py:139
  45.5 5.6 convert_bitcast_fusion.2
  51.7 5.7 convert_bitcast_fusion
  57.4 2.0 all-to-all-done
  65.3 3.2 collective-permute-start
  69.9 5.6 convert_bitcast_fusion.1
  75.5 10.3 %copy.127 = bf16[3,3,10,32,8,32]{5,4,3,2,1,0:T(8,128)(2,1)} copy(bf16[3,3,10,32,8,32]{5,2,3,1,0,4:T(8,128)(2,1)} %convert_bitcast_fusion.2) | data formatting | bytes 2949120 | tf_op jit(solution)/shard_map/convert_element_type | solution.py:28
  85.9 7.2 convert_element_type.66
  93.4 10.3 %copy.141 = bf16[3,3,10,32,8,32]{5,4,3,2,1,0:T(8,128)(2,1)} copy(bf16[3,3,10,32,8,32]{5,2,3,1,0,4:T(8,128)(2,1)} %convert_bitcast_fusion) | data formatting | bytes 2949120 | tf_op jit(solution)/shard_map/convert_element_type | solution.py:28
  103.7 8.3 %convert_element_type.74 = bf16[3,3,320,256]{3,2,1,0:T(8,128)(2,1)} reshape(bf16[3,3,10,32,8,32]{5,4,3,2,1,0:T(8,128)(2,1)} %copy.141) | data formatting | bytes 2949120 | tf_op jit(solution)/shard_map/convert_element_type | solution.py:28
  111.9 10.4 %copy.134 = bf16[3,3,10,32,8,32]{5,4,3,2,1,0:T(8,128)(2,1)} copy(bf16[3,3,10,32,8,32]{5,2,3,1,0,4:T(8,128)(2,1)} %convert_bitcast_fusion.1) | data formatting | bytes 2949120 | tf_op jit(solution)/shard_map/convert_element_type | solution.py:28
  122.3 7.2 convert_element_type.70
  133.8 2.2 gather_fusion.2
  141.8 3.0 scatter.60
  144.8 2.9 scatter.61
  147.7 4.0 scatter.64
  151.7 4.0 scatter.65
  155.7 2.9 scatter.66
  158.7 5.7 scatter.69
  170.1 4.0 collective-permute-start.2
  182.6 2.7 scatter.84
  185.3 2.7 scatter.85
  188.8 5.0 scatter.89
  215.1 2.7 scatter.74
  217.8 2.7 scatter.75
  221.3 5.2 scatter.79
  231.0 2.2 fusion.72
  234.8 2.2 fusion.75
  238.5 2.2 fusion.78
  274.5 2.2 fusion.45
  282.8 464.0 %all-reduce.6.cloned.1.call-done = (f32[27,32,32]{2,1,0:T(8,128)}, f32[27,32,32]{2,1,0:T(8,128)}) async-done(((f32[27,32,32]{2,1,0:T(8,128)}, f32[27,32,32]{2,1,0:T(8,128)}), (f32[27,32,32]{2,1,0:T(8,128)}, f32[27,32,32]{2,1,0:T(8,128)})) %all-reduce.6.cloned.1.call-update) | async-done | bytes 221200 | tf_op jit(solution)/shard_map/psum | solution.py:164
  (269 shorter events, 119.5 us)
Async XLA Ops:
  7.2 16.7 %copy-start = (bf16[1,64,512]{2,1,0:T(8,128)(2,1)S(1)}, bf16[1,64,512]{2,1,0:T(8,128)(2,1)}, u32[]{:S(2)}) copy-start(bf16[1,64,512]{2,1,0:T(8,128)(2,1)} %param.45) | copy-start | bytes 196612
  7.2 38.3 %copy-start.8 = (bf16[27,32,32]{2,1,0:T(8,128)(2,1)S(1)}, bf16[27,32,32]{2,1,0:T(8,128)(2,1)}, u32[]{:S(2)}) copy-start(bf16[27,32,32]{2,1,0:T(8,128)(2,1)} %param.50) | copy-start | bytes 165892
  13.7 162.1 %collective-permute-start.4 = (bf16[1,2,6,2048]{3,1,2,0:T(2,128)(2,1)}, bf16[1,2,6,2048]{3,1,2,0:T(2,128)(2,1)}, u32[]{:S(2)}, u32[]{:S(2)}) collective-permute-start(bf16[1,2,6,2048]{3,1,2,0:T(2,128)(2,1)} %bitcast.92), channel_id=1, source_target_pairs={{0,8},{8,16},{16,24},{24,32},{32,40},{40,48},{48,56},{56,64},{64,7... | collective-permute-start | bytes 147464 | tf_op jit(solution)/shard_map/ppermute | solution.py:12
  18.7 157.2 %collective-permute-start.5 = (bf16[1,2,6,2048]{3,1,2,0:T(2,128)(2,1)}, bf16[1,2,6,2048]{3,1,2,0:T(2,128)(2,1)}, u32[]{:S(2)}, u32[]{:S(2)}) collective-permute-start(bf16[1,2,6,2048]{3,1,2,0:T(2,128)(2,1)} %bitcast.92), channel_id=1, source_target_pairs={{8,0},{16,8},{24,16},{32,24},{40,32},{48,40},{56,48},{64,56},{72,6... | collective-permute-start | bytes 147464 | tf_op jit(solution)/shard_map/ppermute | solution.py:12
  21.3 116.2 %copy-start.16 = (pred[2,6]{1,0:T(4,128)(4,1)}, pred[2,6]{1,0:T(4,128)(4,1)S(1)}, u32[]{:S(2)}) copy-start(pred[2,6]{1,0:T(4,128)(4,1)S(1)} %get-tuple-element.285) | copy-start | bytes 40
  23.8 112.2 %copy-start.14 = (pred[12]{0:T(512)(128)(4,1)}, pred[12]{0:T(512)(128)(4,1)S(1)}, u32[]{:S(2)}) copy-start(pred[12]{0:T(512)(128)(4,1)S(1)} %get-tuple-element.242) | copy-start | bytes 40
  25.9 33.5 %all-to-all-start = ((bf16[64,2,512]{2,1,0:T(2,128)(2,1)}), bf16[64,2,512]{2,1,0:T(2,128)(2,1)S(1)}, u32[]{:S(2)}, u32[]{:S(2)}) async-start(bf16[64,2,512]{2,1,0:T(2,128)(2,1)} %broadcast_select_fusion.1), calls=%async_computation | async-start | bytes 262144 | tf_op jit(solution)/shard_map/all_to_all | solution.py:139
  45.4 701.4 %all-reduce.6.cloned.1.call-start = ((), (), s32[]{:S(2)}) async-start(), calls=%async_computation.1 | async-start | bytes 1769472 | tf_op jit(solution)/shard_map/psum | solution.py:164
  45.5 5.6 copy-start.18
  45.5 5.7 copy-start.9
  45.5 6.0 copy-start.6
  61.2 68.3 %copy-start.4 = (bf16[2,8,8,256]{3,2,1,0:T(8,128)(2,1)}, bf16[2,8,8,256]{3,2,1,0:T(8,128)(2,1)S(1)}, u32[]{:S(2)}) copy-start(bf16[2,8,8,256]{3,2,1,0:T(8,128)(2,1)S(1)} %convert_element_type.62) | copy-start | bytes 196612
  65.3 65.0 %collective-permute-start = (bf16[1,2,6,2048]{3,1,2,0:T(2,128)(2,1)}, bf16[1,2,6,2048]{3,1,2,0:T(2,128)(2,1)}, u32[]{:S(2)}, u32[]{:S(2)}) collective-permute-start(bf16[1,2,6,2048]{3,1,2,0:T(2,128)(2,1)} %bitcast.10), channel_id=1, source_target_pairs={{0,8},{8,16},{16,24},{24,32},{32,40},{40,48},{48,56},{56,64},{64,7... | collective-permute-start | bytes 147464 | tf_op jit(solution)/shard_map/ppermute | solution.py:12
  68.5 61.8 %collective-permute-start.1 = (bf16[1,2,6,2048]{3,1,2,0:T(2,128)(2,1)}, bf16[1,2,6,2048]{3,1,2,0:T(2,128)(2,1)}, u32[]{:S(2)}, u32[]{:S(2)}) collective-permute-start(bf16[1,2,6,2048]{3,1,2,0:T(2,128)(2,1)} %bitcast.10), channel_id=1, source_target_pairs={{8,0},{16,8},{24,16},{32,24},{40,32},{48,40},{56,48},{64,56},{72,6... | collective-permute-start | bytes 147464 | tf_op jit(solution)/shard_map/ppermute | solution.py:12
  85.9 7.2 copy-start.7
  164.3 3.4 copy-start.2
  170.1 7.7 %collective-permute-start.2 = (bf16[1,2,6,2048]{3,1,2,0:T(2,128)(2,1)S(1)}, bf16[1,2,6,2048]{3,1,2,0:T(2,128)(2,1)S(1)}, u32[]{:S(2)}, u32[]{:S(2)}) collective-permute-start(bf16[1,2,6,2048]{3,1,2,0:T(2,128)(2,1)S(1)} %bitcast.663), channel_id=1, source_target_pairs={{0,8},{8,16},{16,24},{24,32},{32,40},{40,48},{48,56},{56,64},{64,7... | collective-permute-start | bytes 147464 | tf_op jit(solution)/shard_map/ppermute | solution.py:12
  174.1 4.8 collective-permute-start.3
  177.0 2.9 copy-start.15
  177.0 3.0 copy-start.17
  196.0 6.7 copy-start.19
  199.3 4.5 copy-start.3
  250.6 1.6 copy-start.10
  250.6 1.6 copy-start.11
  250.6 1.6 copy-start.12
  277.9 1.6 copy-start.13
  281.2 0.8 copy-start.5
  281.9 468.5 %copy-start.1 = (bf16[1,64,512]{2,1,0:T(8,128)(2,1)S(1)}, bf16[1,64,512]{2,1,0:T(8,128)(2,1)}, u32[]{:S(2)}) copy-start(bf16[1,64,512]{2,1,0:T(8,128)(2,1)} %param.45) | copy-start | bytes 196612
Sparse Core Ops, SparseCore 0:
  282.1 464.6 all-reduce.5
where the time goes:
time: 765 us; the launch traced here: 757 us
  waiting for transfers between devices  467 us (61%)
  local copies, waits for them, and re-layouts  151 us (20%)
  matrix products  78.1 us (10%)
  starting transfers between devices  36.2 us (5%)
  between operations  15.5 us (2%)
  other arithmetic  9.85 us (1%)
    psum x1, waiting for transfers between devices, body(): grad_one, grad_two = lax.psum((first_local, second_local), ('space', 'dp'))  464 us
    convert_element_type x6, local copies, waits for them, and re-layouts, band_matrix(): banded.reshape(3, 3, (extent + 2) * channels, extent * channels)  53.6 us
    dot_general x18, matrix products, band_gradient(): jnp.einsum('dpq,piqo->dio', select, outer, precision=lax.Precision.HIGHEST)  30.9 us
    all_to_all x1, starting transfers between devices, body(): lax.all_to_all(packed, 'space', split_axis=0, concat_axis=0, tiled=True)  19.5 us
    dot_general x27, matrix products, apply_band(): jnp.einsum('nxyp,pq->nxyq', window, banded[shift_x, shift_y], preferred_e...  17.4 us
    dot_general x3, matrix products, band_matrix(): jnp.einsum('dpq,abdio->abpiqo', depth_select(extent), cube, precision=lax...  16.8 us
    ppermute x6, starting transfers between devices, passed_along(): lax.ppermute(value, axis, [(source, source + steps) for source in range(f...  16.6 us
    scatter x3, local copies, waits for them, and re-layouts, fill_padding(): padded.at[:, inside_range, inside_range, (extent + 1) * channels:]  15.9 us
  transfers between devices with their start and end apart: 8, of which 3 were waited for; matrix products, arithmetic and copies ran while one was open for 17% of the time, Pallas kernels for 0%

commit v1 on v0

v1 whole, which is shorter than its diff:
```python
import math

import jax
import jax.numpy as jnp
from jax import lax
from jax.experimental import pallas as pl
from jax.experimental.pallas import tpu as pltpu
from jax.sharding import PartitionSpec as P

MESH_ID = pl.DeviceIdType.MESH
F32 = jnp.float32
BF16 = jnp.bfloat16


def iota(shape, dim):
    return lax.broadcasted_iota(jnp.int32, shape, dim)


def picked_rows(active_ref, coarse_ref, position):
    rows = 528
    group = ((iota((rows, 128), 0) >> 2) + 126) & 127
    listed = active_ref[...].astype(F32)
    mine = jnp.where(group == iota((rows, 128), 1), listed, 0.0)
    column = jnp.sum(mine, axis=1, keepdims=True)
    local = column - (position * 64).astype(F32)
    quarter = ((iota((rows, 256), 0) & 3) * 64).astype(F32)
    held = (local >= 0.0) & (local < 64.0)
    target = jnp.where(held, local, -1000.0) + quarter
    chosen = jnp.where(iota((rows, 256), 1).astype(F32) == target, 1.0, 0.0).astype(BF16)
    source = jnp.concatenate([coarse_ref[:, k * 128 : (k + 1) * 128] for k in range(4)], axis=0)
    return jnp.dot(chosen, source, preferred_element_type=F32)


def repeat_weights(weight_ref):
    pattern = jnp.where((iota((32, 256), 1) & 31) == iota((32, 256), 0), 1.0, 0.0).astype(BF16)
    return jnp.dot(weight_ref[...], pattern, preferred_element_type=F32)


def fill_band(band_ref, rep_ref):
    block = iota((32, 256), 1) >> 5
    for a in range(3):
        for b in range(3):
            base = (a * 3 + b) * 96
            low = rep_ref[base : base + 32, :]
            mid = rep_ref[base + 32 : base + 64, :]
            high = rep_ref[base + 64 : base + 96, :]
            for zi in range(8):
                strip = jnp.where(block == zi - 1, high, 0.0)
                strip = jnp.where(block == zi, mid, strip)
                strip = jnp.where(block == zi + 1, low, strip)
                first = b * 256 + zi * 32
                band_ref[a, first : first + 32, :] = strip.astype(BF16)
            first = 768 + b * 64
            band_ref[a, first : first + 32, :] = jnp.where(block == 0, low, 0.0).astype(BF16)
            band_ref[a, first + 32 : first + 64, :] = jnp.where(block == 7, high, 0.0).astype(BF16)
        band_ref[a, 960:1024, :] = jnp.zeros((64, 256), BF16)


def fill_band_back(band_ref, rep_ref):
    block = iota((32, 256), 1) >> 5
    for a in range(3):
        faces_first = jnp.zeros((32, 256), F32)
        faces_last = jnp.zeros((32, 256), F32)
        for b in range(3):
            base = ((2 - a) * 3 + 2 - b) * 96
            low = rep_ref[base : base + 32, :]
            mid = rep_ref[base + 32 : base + 64, :]
            high = rep_ref[base + 64 : base + 96, :]
            for zo in range(8):
                strip = jnp.where(block == zo + 1, low, 0.0)
                strip = jnp.where(block == zo, mid, strip)
                strip = jnp.where(block == zo - 1, high, strip)
                band_ref[a, zo * 32 : zo * 32 + 32, b * 256 : b * 256 + 256] = strip.astype(BF16)
            faces_first = jnp.where(block == 2 * b, high, faces_first)
            faces_last = jnp.where(block == 2 * b + 1, low, faces_last)
        band_ref[a, 0:32, 768:1024] = faces_first.astype(BF16)
        band_ref[a, 32:224, 768:1024] = jnp.zeros((192, 256), BF16)
        band_ref[a, 224:256, 768:1024] = faces_last.astype(BF16)


def fill_lift(lift_ref, up_ref):
    lift_ref[...] = jnp.zeros((512, 1024), BF16)
    for ky in range(4):
        for kx in range(4):
            part = up_ref[:, (kx * 4 + ky) * 128 : (kx * 4 + ky + 1) * 128]
            for c in range(2):
                row = ky * 128 + c * 64
                lane = kx * 256 + c * 128
                lift_ref[row : row + 64, lane : lane + 128] = part


def chosen_neighbour(links_ref, position, brick, face, before, own, after):
    link = links_ref[brick, face]
    if face % 2 == 0:
        outer, first = before, jnp.where(position > 0, 2 * position - 2, -8)
    else:
        outer, first = after, 2 * position + 2
    total = None
    for slices, base in ((outer, first), (own, 2 * position)):
        for m in range(2):
            mask = jnp.where(link == base + m, 1.0, 0.0).astype(F32)
            term = slices[m] * mask
            total = term if total is None else total + term
    return total


def fill_windows(win_ref, links_ref, position, before, own, after):
    row = iota((8, 8, 256), 1)
    row_face = iota((8, 256), 0)
    lane = iota((8, 8, 128), 2)
    row_half = iota((8, 8, 128), 1)
    shifted = []
    faces = []
    for n in range(2):
        volume = own(n)

        def neighbour(face, part):
            sources = [[part(f, m) for m in range(2)] for f in (before, own, after)]
            return chosen_neighbour(links_ref, position, n, face, *sources)

        y_minus = neighbour(2, lambda f, m: f(m)[:, 7:8, :])
        y_plus = neighbour(3, lambda f, m: f(m)[:, 0:1, :])
        back_one = jnp.where(row == 0, y_minus, pltpu.roll(volume, 1, 1))
        ahead_one = jnp.where(row == 7, y_plus, pltpu.roll(volume, 7, 1))
        z_minus = neighbour(4, lambda f, m: f(m)[:, :, 128:256])
        z_plus = neighbour(5, lambda f, m: f(m)[:, :, 0:128])
        pair = pltpu.roll(jnp.where(lane >= 64, z_minus, z_plus), 32, 2)
        pair = jnp.where(lane < 64, pair, 0.0)
        first = jnp.where(row_half == 0, 0.0, pltpu.roll(pair, 1, 1)) + pltpu.roll(pair, 64, 2)
        second = jnp.where(row_half == 7, 0.0, pltpu.roll(pair, 7, 1))
        shifted.append((back_one, volume, ahead_one, first, second))
        ends = []
        for face, x in ((0, 7), (1, 0)):
            plane = neighbour(face, lambda f, m: f(m)[x])
            ends.append(
                (
                    jnp.where(row_face == 0, 0.0, pltpu.roll(plane, 1, 0)),
                    plane,
                    jnp.where(row_face == 7, 0.0, pltpu.roll(plane, 7, 0)),
                )
            )
        faces.append(ends)
    for k in range(5):
        both = jnp.concatenate([shifted[0][k], shifted[1][k]], axis=1).astype(BF16)
        first = k * 256 if k < 4 else 896
        win_ref[1:9, :, first : first + both.shape[2]] = both
    for end, x in ((0, 0), (1, 9)):
        for k in range(3):
            both = jnp.concatenate([faces[0][end][k], faces[1][end][k]], axis=0)
            win_ref[x, :, k * 256 : k * 256 + 256] = both.astype(BF16)
        win_ref[x, :, 768:1024] = jnp.zeros((16, 256), BF16)


def window(win_ref, a):
    return win_ref[a : a + 8].reshape(128, 1024)


def convolve(win_ref, band_ref):
    total = None
    for a in range(3):
        term = jnp.dot(window(win_ref, a), band_ref[a], preferred_element_type=F32)
        total = term if total is None else total + term
    return total


def convolve_back(win_ref, band_ref):
    total = None
    for a in range(3):
        term = lax.dot_general(
            window(win_ref, a), band_ref[a], (((1,), (1,)), ((), ())), preferred_element_type=F32
        )
        total = term if total is None else total + term
    return total


def weight_products(turned, win_ref, parts_ref, first_part, reverse):
    block = iota((32, 256), 1) >> 5
    block_half = iota((32, 128), 1) >> 5
    sums = [None] * 28
    sums[27] = jnp.zeros((32, 128), F32)
    for a in range(3):
        seen = window(win_ref, a)
        faces = jnp.dot(turned, seen[:, 768:1024], preferred_element_type=F32)
        for b in range(3):
            outer = jnp.dot(turned, seen[:, b * 256 : b * 256 + 256], preferred_element_type=F32)
            half = (b // 2) * 128
            for dz in range(3):
                total = None
                for z in range(8):
                    zi = z + dz - 1
                    if 0 <= zi < 8:
                        side = slice(0, 128) if zi < 4 else slice(128, 256)
                        strip = outer[z * 32 : z * 32 + 32, side]
                        term = jnp.where(block_half == zi % 4, strip, 0.0)
                        total = term if total is None else total + term
                if dz == 0:
                    strip = faces[0:32, half : half + 128]
                    total = total + jnp.where(block_half == (2 * b) % 4, strip, 0.0)
                if dz == 2:
                    strip = faces[224:256, half : half + 128]
                    total = total + jnp.where(block_half == (2 * b + 1) % 4, strip, 0.0)
                total = total + pltpu.roll(total, 64, 1)
                total = total + pltpu.roll(total, 32, 1)
                index = (a * 3 + b) * 3 + dz
                sums[26 - index if reverse else index] = total
    for k in range(7):
        packed = sums[4 * k]
        for j in range(1, 4):
            packed = jnp.where(block_half == j, sums[4 * k + j], packed)
        parts_ref[first_part + 2 * k] = packed[0:16]
        parts_ref[first_part + 2 * k + 1] = packed[16:32]


def step_kernel(
    coarse_ref,
    active_ref,
    links_ref,
    cot_ref,
    up_ref,
    one_ref,
    two_ref,
    fine_ref,
    grad_one_ref,
    grad_two_ref,
    pack_ref,
    y_buf,
    y_sum,
    high_buf,
    high_sum,
    low_buf,
    cot_buf,
    hid_ref,
    hid_buf,
    rep_one,
    rep_two,
    band_one,
    band_two,
    band_back,
    lift_ref,
    lifted_ref,
    win_cot,
    win_lift,
    win_hid,
    parts_ref,
    first_buf,
    near_buf,
    far_buf,
    total_ref,
    send_sems,
    recv_sems,
):
    position = lax.axis_index("space")
    dp = lax.axis_index("dp")
    row, depth = position // 16, position % 16
    low, high = depth % 4, depth // 4
    me = row * 8 + dp

    def wide(step):
        other = (me + step) % 32
        return other, {"space": (other // 8) * 16 + depth, "dp": other % 8}

    def along_y(step):
        other = (row + step) % 4
        return other, {"space": other * 16 + depth, "dp": dp}

    def near(step):
        other = (low + step) % 4
        return other, {"space": row * 16 + high * 4 + other, "dp": dp}

    def far(step):
        other = (high + step) % 4
        return other, {"space": row * 16 + other * 4 + low, "dp": dp}

    after = {"space": (position + 1) % 64, "dp": dp}
    before = {"space": (position + 63) % 64, "dp": dp}

    barrier = pltpu.get_barrier_semaphore()
    for step in range(1, 4):
        pl.semaphore_signal(barrier, inc=1, device_id=near(step)[1], device_id_type=MESH_ID)
        pl.semaphore_signal(barrier, inc=1, device_id=far(step)[1], device_id_type=MESH_ID)
    pl.semaphore_signal(barrier, inc=1, device_id=after, device_id_type=MESH_ID)
    pl.semaphore_signal(barrier, inc=1, device_id=before, device_id_type=MESH_ID)
    for step in range(1, 32):
        pl.semaphore_signal(barrier, inc=1, device_id=wide(step)[1], device_id_type=MESH_ID)

    def send(source, target, device, phase):
        pltpu.make_async_remote_copy(
            src_ref=source,
            dst_ref=target,
            send_sem=send_sems.at[phase],
            recv_sem=recv_sems.at[phase],
            device_id=device,
            device_id_type=MESH_ID,
        ).start()

    def finish(part, phase):
        pltpu.make_async_copy(part, part, recv_sems.at[phase]).wait()

    def sent(part, phase):
        pltpu.make_async_copy(part, part, send_sems.at[phase]).wait()

    pack_ref[...] = picked_rows(active_ref, coarse_ref, position).astype(BF16)
    pl.semaphore_wait(barrier, 39)

    for step in range(1, 4):
        other, device = along_y(step)
        start = pl.multiple_of(other * 128, 128)
        send(pack_ref.at[pl.ds(start, 144)], y_buf.at[row], device, 0)
    send(cot_ref, cot_buf.at[0], after, 3)
    send(cot_ref, cot_buf.at[1], before, 3)
    fill_lift(lift_ref, up_ref)
    rep_two[...] = repeat_weights(two_ref)
    fill_band_back(band_back, rep_two)
    finish(y_buf.at[pl.ds(0, 3)], 0)
    total = pack_ref[pl.ds(pl.multiple_of(row * 128, 128), 144)].astype(F32)
    for step in range(1, 4):
        total = total + y_buf[(row + step) % 4].astype(F32)
    y_sum[...] = total.astype(BF16)
    for step in range(1, 4):
        other, device = far(step)
        start = pl.multiple_of(other * 32, 32)
        send(y_sum.at[pl.ds(start, 48)], high_buf.at[high], device, 1)
    rep_one[...] = repeat_weights(one_ref)
    fill_band(band_one, rep_one)
    finish(high_buf.at[pl.ds(0, 3)], 1)
    total = y_sum[pl.ds(pl.multiple_of(high * 32, 32), 48)].astype(F32)
    for step in range(1, 4):
        total = total + high_buf[(high + step) % 4].astype(F32)
    high_sum[...] = total
    for step in range(1, 4):
        other, device = near(step)
        start = pl.multiple_of(other * 8, 8)
        send(high_sum.at[pl.ds(start, 24)], low_buf.at[low], device, 2)

    finish(cot_buf, 3)

    def cot_before(n):
        return cot_buf[0, n * 64 : n * 64 + 64].astype(F32).reshape(8, 8, 256)

    def cot_own(n):
        return cot_ref[n * 64 : n * 64 + 64].astype(F32).reshape(8, 8, 256)

    def cot_after(n):
        return cot_buf[1, n * 64 : n * 64 + 64].astype(F32).reshape(8, 8, 256)

    fill_windows(win_cot, links_ref, position, cot_before, cot_own, cot_after)
    back = convolve_back(win_cot, band_back)
    finish(low_buf.at[pl.ds(0, 3)], 2)

    rows = high_sum[pl.ds(pl.multiple_of(low * 8, 8), 24)]
    for step in range(1, 4):
        rows = rows + low_buf[(low + step) % 4]
    y_index = iota((8, 128), 0)
    pieces = []
    for j in range(3):
        for a in range(2):
            for n in range(2):
                at = j * 8 + n * 4 + a * 2
                near_half = jnp.broadcast_to(rows[at : at + 1], (8, 128))
                far_half = jnp.broadcast_to(rows[at + 1 : at + 2], (8, 128))
                cell = jnp.where(y_index < 4, near_half, far_half)
                pieces.append(
                    jnp.concatenate(
                        [jnp.where((y_index & 3) == ky, cell, 0.0) for ky in range(4)], axis=1
                    )
                )
    cells = jnp.concatenate(pieces, axis=0).astype(BF16)
    lifted = jnp.dot(cells, lift_ref[...], preferred_element_type=F32).astype(BF16).astype(F32)
    for j in range(3):
        for a in range(2):
            for kx in range(4):
                part = lifted[j * 32 + a * 16 : j * 32 + a * 16 + 16, kx * 256 : kx * 256 + 256]
                lifted_ref[j, a * 4 + kx] = part

    def lifted_of(j):
        return lambda n: lifted_ref[j, :, n * 8 : n * 8 + 8, :]

    fill_windows(win_lift, links_ref, position, lifted_of(0), lifted_of(1), lifted_of(2))
    pre = convolve(win_lift, band_one)
    sigmoid = 1.0 / (1.0 + jnp.exp(-pre))
    hidden = (pre * sigmoid).astype(BF16)
    hid_ref[...] = hidden
    send(hid_ref, hid_buf.at[0], after, 4)
    send(hid_ref, hid_buf.at[1], before, 4)
    grad_pre = (back * sigmoid * (1.0 + pre * (1.0 - sigmoid))).astype(BF16)

    turned_hidden = jnp.transpose(hidden.astype(F32)).astype(BF16)
    turned_grad = jnp.transpose(grad_pre.astype(F32)).astype(BF16)
    weight_products(turned_hidden, win_cot, parts_ref, 14, True)
    weight_products(turned_grad, win_lift, parts_ref, 0, False)
    for k in range(28, 32):
        parts_ref[k] = jnp.zeros((16, 128), F32)

    for step in range(1, 32):
        other, device = wide(step)
        send(parts_ref.at[other], first_buf.at[me], device, 5)
    fill_band(band_two, rep_two)
    finish(first_buf.at[pl.ds(0, 31)], 5)
    first_buf[me] = parts_ref[me]
    near_buf[low] = jnp.sum(first_buf[...], axis=0)
    for step in range(1, 4):
        send(near_buf.at[low], near_buf.at[low], near(step)[1], 6)
    finish(hid_buf, 4)

    def hid_of(ref):
        def part(n):
            return ref[...].astype(F32).reshape(8, 16, 256)[:, n * 8 : n * 8 + 8, :]

        return part

    fill_windows(
        win_hid, links_ref, position, hid_of(hid_buf.at[0]), hid_of(hid_ref), hid_of(hid_buf.at[1])
    )
    finish(near_buf.at[pl.ds(0, 3)], 6)
    far_buf[high] = (near_buf[0] + near_buf[1]) + (near_buf[2] + near_buf[3])
    for step in range(1, 4):
        send(far_buf.at[high], far_buf.at[high], far(step)[1], 7)
    second = convolve(win_hid, band_two)
    scale = 1.0 / math.sqrt(8 * 128 * 512)
    finish(far_buf.at[pl.ds(0, 3)], 7)
    total_ref[me] = ((far_buf[0] + far_buf[1]) + (far_buf[2] + far_buf[3])) * scale
    for step in range(1, 32):
        send(total_ref.at[me], total_ref.at[me], wide(step)[1], 8)
    fine = second.reshape(8, 16, 256) + lifted_ref[1]
    for n in range(2):
        fine_ref[n * 64 : n * 64 + 64] = fine[:, n * 8 : n * 8 + 8, :].reshape(64, 256).astype(BF16)
    finish(total_ref.at[pl.ds(0, 31)], 8)

    for k in range(7):
        packed = total_ref[2 * k : 2 * k + 2].reshape(32, 128)
        turned = jnp.transpose(packed).reshape(4, 32, 32)
        count = min(4, 27 - 4 * k)
        grad_one_ref[4 * k : 4 * k + count] = turned[0:count]
        packed = total_ref[14 + 2 * k : 14 + 2 * k + 2].reshape(32, 128)
        for j in range(count):
            moved = packed if j == 0 else pltpu.roll(packed, 128 - 32 * j, 1)
            grad_two_ref[4 * k + j] = moved[:, 0:32]

    sent(y_buf.at[pl.ds(0, 3)], 0)
    sent(high_buf.at[pl.ds(0, 3)], 1)
    sent(low_buf.at[pl.ds(0, 3)], 2)
    sent(cot_buf, 3)
    sent(hid_buf, 4)
    sent(first_buf.at[pl.ds(0, 31)], 5)
    sent(near_buf.at[pl.ds(0, 3)], 6)
    sent(far_buf.at[pl.ds(0, 3)], 7)
    sent(total_ref.at[pl.ds(0, 31)], 8)


def body(coarse_latents, active_blocks, face_links, cotangent, up_weight, conv_one, conv_two):
    vmem = pl.BlockSpec(memory_space=pltpu.VMEM)
    smem = pl.BlockSpec(memory_space=pltpu.SMEM)
    scratch = [
        ((528, 128), BF16),
        ((4, 144, 128), BF16),
        ((144, 128), BF16),
        ((4, 48, 128), BF16),
        ((48, 128), F32),
        ((4, 24, 128), F32),
        ((2, 128, 256), BF16),
        ((128, 256), BF16),
        ((2, 128, 256), BF16),
        ((864, 256), F32),
        ((864, 256), F32),
        ((3, 1024, 256), BF16),
        ((3, 1024, 256), BF16),
        ((3, 256, 1024), BF16),
        ((512, 1024), BF16),
        ((3, 8, 16, 256), F32),
        ((10, 16, 1024), BF16),
        ((10, 16, 1024), BF16),
        ((10, 16, 1024), BF16),
        ((32, 16, 128), F32),
        ((32, 16, 128), F32),
        ((4, 16, 128), F32),
        ((4, 16, 128), F32),
        ((32, 16, 128), F32),
    ]
    fine, grad_one, grad_two = pl.pallas_call(
        step_kernel,
        out_shape=(
            jax.ShapeDtypeStruct((128, 256), BF16),
            jax.ShapeDtypeStruct((27, 32, 32), F32),
            jax.ShapeDtypeStruct((27, 32, 32), F32),
        ),
        in_specs=[vmem, vmem, smem, vmem, vmem, vmem, vmem],
        out_specs=(vmem, vmem, vmem),
        scratch_shapes=[pltpu.VMEM(*one) for one in scratch]
        + [pltpu.SemaphoreType.DMA((9,)), pltpu.SemaphoreType.DMA((9,))],
        compiler_params=pltpu.CompilerParams(
            collective_id=0, has_side_effects=True, vmem_limit_bytes=40 * 1024 * 1024
        ),
    )(
        coarse_latents[0],
        active_blocks,
        face_links[0],
        cotangent.reshape(128, 256),
        up_weight,
        conv_one.reshape(864, 32),
        conv_two.reshape(864, 32),
    )
    return fine.reshape(1, 2, 8, 8, 256), grad_one, grad_two


def solution(mesh):
    return jax.shard_map(
        body,
        mesh=mesh,
        in_specs=(
            P("dp", "space", None),
            P("dp", None),
            P("dp", "space", None),
            P("dp", "space", None, None, None),
            P(),
            P(),
            P(),
        ),
        out_specs=(P("dp", "space", None, None, None), P(), P()),
        check_vma=False,
    )
```

time: 765 us -> 66.4 us (0.09)
  waiting for transfers between devices: 467 us -> 0 us
  local copies, waits for them, and re-layouts: 151 us -> 7.32 us
  matrix products: 78.1 us -> 0 us
  Pallas kernels: 0 us -> 58.1 us
  starting transfers between devices: 36.2 us -> 0 us
  between operations: 15.5 us -> 0.66 us
  other arithmetic: 9.85 us -> 0 us
    psum x1 -> x0, waiting for transfers between devices: 464 us -> none  [body(): grad_one, grad_two = lax.psum((first_local, second_local), ('space', 'dp'))]
    dot_general x67 -> x0, matrix products: 78.1 us -> none  [the longest x18 30.9 us: band_gradient(): jnp.einsum('dpq,piqo->dio', select, outer, precision=lax.Precision.HIGHEST)]
    pallas_call x0 -> x1, Pallas kernels: none -> 58.1 us  [body(): pl.pallas_call(step_kernel, out_shape=(jax.ShapeDtypeStruct((128, 256), B...]
    convert_element_type x8 -> x0, local copies, waits for them, and re-layouts: 53.9 us -> none  [the longest x6 53.6 us: band_matrix(): banded.reshape(3, 3, (extent + 2) * channels, extent * channels)]
    scatter x18 -> x0, local copies, waits for them, and re-layouts: 49 us -> none  [the longest x3 15.9 us: fill_padding(): padded.at[:, inside_range, inside_range, (extent + 1) * channels:]]
    all_to_all x1 -> x0, starting transfers between devices: 19.5 us -> none  [body(): lax.all_to_all(packed, 'space', split_axis=0, concat_axis=0, tiled=True)]
    ppermute x6 -> x0, starting transfers between devices: 16.6 us -> none  [passed_along(): lax.ppermute(value, axis, [(source, source + steps) for source in range(f...]
    reshape x13 -> x0, local copies, waits for them, and re-layouts: 12.5 us -> none  [the longest x9 11.6 us: band_gradient(): outer = outer.reshape(extent + 2, channels, extent, channels)]
  transfers between devices with their start and end apart: 8 -> 0, of which waited for: 3 -> 0; matrix products, arithmetic and copies ran while one was open for 17% -> 0% of each run, Pallas kernels for 0% -> 0%
where the time goes in v1:
time: 66.4 us; the launch traced here: 66.1 us
  Pallas kernels  58.1 us (87%)
  local copies, waits for them, and re-layouts  7.32 us (11%)
    pallas_call x1, Pallas kernels, body(): pl.pallas_call(step_kernel, out_shape=(jax.ShapeDtypeStruct((128, 256), B...  58.1 us
    unnamed x17, local copies, waits for them, and re-layouts  7.32 us

profile of v1, /device:TPU:1, one launch (start us, length us, event | category | flops | bytes accessed | tf_op | source)
XLA Modules:
  0.0 66.1 jit_solution(16756816925890843271)
XLA Ops:
  0.6 0.0 copy-start.5
  0.6 0.0 copy-start.6
  0.7 0.7 copy-done.5
  1.3 0.0 copy-done.6
  1.3 0.0 copy-start
  1.3 0.9 %copy-done = bf16[64,2048]{1,0:T(8,128)(2,1)S(1)} copy-done((bf16[64,2048]{1,0:T(8,128)(2,1)S(1)}, bf16[64,2048]{1,0:T(8,128)(2,1)}, u32[]{:S(2)}) %copy-start) | copy-done | bytes 262168
  2.3 0.0 copy-start.1
  2.3 0.9 %copy-done.1 = bf16[27,32,32]{2,1,0:T(8,128)(2,1)S(1)} copy-done((bf16[27,32,32]{2,1,0:T(8,128)(2,1)S(1)}, bf16[27,32,32]{2,1,0:T(8,128)(2,1)}, u32[]{:S(2)}) %copy-start.1) | copy-done | bytes 55320
  3.2 0.0 copy-start.2
  3.2 0.9 %copy-done.2 = bf16[27,32,32]{2,1,0:T(8,128)(2,1)S(1)} copy-done((bf16[27,32,32]{2,1,0:T(8,128)(2,1)S(1)}, bf16[27,32,32]{2,1,0:T(8,128)(2,1)}, u32[]{:S(2)}) %copy-start.2) | copy-done | bytes 55320
  4.1 0.0 copy-start.3
  4.1 0.8 %copy-done.3 = bf16[1,64,512]{2,1,0:T(8,128)(2,1)S(1)} copy-done((bf16[1,64,512]{2,1,0:T(8,128)(2,1)S(1)}, bf16[1,64,512]{2,1,0:T(8,128)(2,1)}, u32[]{:S(2)}) %copy-start.3) | copy-done | bytes 65560
  5.0 0.0 copy-start.4
  5.0 0.8 %copy-done.4 = bf16[1,2,8,8,256]{4,3,2,1,0:T(8,128)(2,1)S(1)} copy-done((bf16[1,2,8,8,256]{4,3,2,1,0:T(8,128)(2,1)S(1)}, bf16[1,2,8,8,256]{4,3,2,1,0:T(8,128)(2,1)}, u32[]{:S(2)}) %copy-start.4) | copy-done | bytes 65560
  5.8 58.1 %shard_map.94 = (bf16[128,256]{1,0:T(8,128)(2,1)S(1)}, f32[27,32,32]{2,1,0:T(8,128)S(1)}, f32[27,32,32]{2,1,0:T(8,128)S(1)}) custom-call(bf16[64,512]{1,0:T(8,128)(2,1)S(1)} %bitcast.8, s32[1,128]{1,0:T(1,128)S(1)} %copy-done.6, s32[2,6]{1,0:T(2,128)S(1)} %bitcast.11, bf16[128,256]{1,0:T(8,128)(2,1)S(1)} %bitcast.9, bf16[64,2048]{1,0:T(8,128)(2,1)S(1)} %copy-done, ...), custom_call_target="tpu_custom_call" | custom-call | tf_op jit(solution)/shard_map/pallas_call | solution.py:479
  63.9 0.6 copy.13
  64.5 0.8 %copy.14 = f32[27,32,32]{2,1,0:T(8,128)} copy(f32[27,32,32]{2,1,0:T(8,128)S(1)} %get-tuple-element.13) | data formatting | bytes 221184
  65.3 0.8 %copy.15 = f32[27,32,32]{2,1,0:T(8,128)} copy(f32[27,32,32]{2,1,0:T(8,128)S(1)} %get-tuple-element.14) | data formatting | bytes 221184
Async XLA Ops:
  0.6 0.7 %copy-start.5 = (s32[1,2,6]{2,1,0:T(2,128)S(1)}, s32[1,2,6]{2,1,0:T(2,128)}, u32[]{:S(2)}) copy-start(s32[1,2,6]{2,1,0:T(2,128)} %param.9) | copy-start | bytes 148
  0.6 0.7 %copy-start.6 = (s32[1,128]{1,0:T(1,128)S(1)}, s32[1,128]{1,0:T(1,128)}, u32[]{:S(2)}) copy-start(s32[1,128]{1,0:T(1,128)} %active_ref.1) | copy-start | bytes 1540
  1.3 1.0 %copy-start = (bf16[64,2048]{1,0:T(8,128)(2,1)S(1)}, bf16[64,2048]{1,0:T(8,128)(2,1)}, u32[]{:S(2)}) copy-start(bf16[64,2048]{1,0:T(8,128)(2,1)} %up_ref.1) | copy-start | bytes 786436
  2.3 0.9 %copy-start.1 = (bf16[27,32,32]{2,1,0:T(8,128)(2,1)S(1)}, bf16[27,32,32]{2,1,0:T(8,128)(2,1)}, u32[]{:S(2)}) copy-start(bf16[27,32,32]{2,1,0:T(8,128)(2,1)} %param.12) | copy-start | bytes 165892
  3.2 0.9 %copy-start.2 = (bf16[27,32,32]{2,1,0:T(8,128)(2,1)S(1)}, bf16[27,32,32]{2,1,0:T(8,128)(2,1)}, u32[]{:S(2)}) copy-start(bf16[27,32,32]{2,1,0:T(8,128)(2,1)} %param.13) | copy-start | bytes 165892
  4.1 0.8 %copy-start.3 = (bf16[1,64,512]{2,1,0:T(8,128)(2,1)S(1)}, bf16[1,64,512]{2,1,0:T(8,128)(2,1)}, u32[]{:S(2)}) copy-start(bf16[1,64,512]{2,1,0:T(8,128)(2,1)} %param.7) | copy-start | bytes 196612
  5.0 0.8 %copy-start.4 = (bf16[1,2,8,8,256]{4,3,2,1,0:T(8,128)(2,1)S(1)}, bf16[1,2,8,8,256]{4,3,2,1,0:T(8,128)(2,1)}, u32[]{:S(2)}) copy-start(bf16[1,2,8,8,256]{4,3,2,1,0:T(8,128)(2,1)} %param.10) | copy-start | bytes 196612

commit v2 on v1

--- a/solution.py
+++ b/solution.py
@@ -212,6 +212,15 @@
 
 
 def step_kernel(
+    coarse_in,
+    active_in,
+    links_in,
+    cot_in,
+    up_in,
+    one_in,
+    two_in,
+    fine_ref,
+    sums_ref,
     coarse_ref,
     active_ref,
     links_ref,
@@ -219,12 +228,11 @@
     up_ref,
     one_ref,
     two_ref,
-    fine_ref,
-    grad_one_ref,
-    grad_two_ref,
     pack_ref,
     y_buf,
     y_sum,
+    cross_buf,
+    cross_sum,
     high_buf,
     high_sum,
     low_buf,
@@ -244,10 +252,12 @@
     parts_ref,
     first_buf,
     near_buf,
+    far_own,
     far_buf,
     total_ref,
     send_sems,
     recv_sems,
+    copy_sems,
 ):
     position = lax.axis_index("space")
     dp = lax.axis_index("dp")
@@ -267,21 +277,44 @@
         other = (low + step) % 4
         return other, {"space": row * 16 + high * 4 + other, "dp": dp}
 
-    def far(step):
-        other = (high + step) % 4
-        return other, {"space": row * 16 + other * 4 + low, "dp": dp}
-
-    after = {"space": (position + 1) % 64, "dp": dp}
-    before = {"space": (position + 63) % 64, "dp": dp}
+    def far(other):
+        return {"space": row * 16 + other * 4 + low, "dp": dp}
+
+    half, odd = high // 2, high % 2
+    across = far(3 - high)
+    beside = far(high + 1 - 2 * odd)
+    after = {"space": position + 1, "dp": dp}
+    before = {"space": position - 1, "dp": dp}
+    has_after, has_before = position < 63, position > 0
 
     barrier = pltpu.get_barrier_semaphore()
+    def greet(device):
+        pl.semaphore_signal(barrier, inc=1, device_id=device, device_id_type=MESH_ID)
+
+    greet(across)
+    greet(beside)
+
+    @pl.when(has_after)
+    def _():
+        greet(after)
+
+    @pl.when(has_before)
+    def _():
+        greet(before)
+
     for step in range(1, 4):
-        pl.semaphore_signal(barrier, inc=1, device_id=near(step)[1], device_id_type=MESH_ID)
-        pl.semaphore_signal(barrier, inc=1, device_id=far(step)[1], device_id_type=MESH_ID)
-    pl.semaphore_signal(barrier, inc=1, device_id=after, device_id_type=MESH_ID)
-    pl.semaphore_signal(barrier, inc=1, device_id=before, device_id_type=MESH_ID)
+        greet(near(step)[1])
     for step in range(1, 32):
-        pl.semaphore_signal(barrier, inc=1, device_id=wide(step)[1], device_id_type=MESH_ID)
+        greet(wide(step)[1])
+
+    sources = (coarse_in, active_in, cot_in, links_in, two_in, up_in, one_in)
+    targets = (coarse_ref, active_ref, cot_ref, links_ref, two_ref, up_ref, one_ref)
+    fetches = [
+        pltpu.make_async_copy(source, target, copy_sems.at[k])
+        for k, (source, target) in enumerate(zip(sources, targets))
+    ]
+    for fetch in fetches:
+        fetch.start()
 
     def send(source, target, device, phase):
         pltpu.make_async_remote_copy(
@@ -299,15 +332,28 @@
     def sent(part, phase):
         pltpu.make_async_copy(part, part, send_sems.at[phase]).wait()
 
+    fetches[0].wait()
+    fetches[1].wait()
     pack_ref[...] = picked_rows(active_ref, coarse_ref, position).astype(BF16)
-    pl.semaphore_wait(barrier, 39)
+    fetches[2].wait()
+    partners = 36 + jnp.where(has_after, 1, 0) + jnp.where(has_before, 1, 0)
+    pl.semaphore_wait(barrier, partners)
 
     for step in range(1, 4):
         other, device = along_y(step)
         start = pl.multiple_of(other * 128, 128)
         send(pack_ref.at[pl.ds(start, 144)], y_buf.at[row], device, 0)
-    send(cot_ref, cot_buf.at[0], after, 3)
-    send(cot_ref, cot_buf.at[1], before, 3)
+
+    @pl.when(has_after)
+    def _():
+        send(cot_ref, cot_buf.at[0], after, 3)
+
+    @pl.when(has_before)
+    def _():
+        send(cot_ref, cot_buf.at[1], before, 9)
+
+    for fetch in fetches[3:]:
+        fetch.wait()
     fill_lift(lift_ref, up_ref)
     rep_two[...] = repeat_weights(two_ref)
     fill_band_back(band_back, rep_two)
@@ -316,34 +362,48 @@
     for step in range(1, 4):
         total = total + y_buf[(row + step) % 4].astype(F32)
     y_sum[...] = total.astype(BF16)
-    for step in range(1, 4):
-        other, device = far(step)
-        start = pl.multiple_of(other * 32, 32)
-        send(y_sum.at[pl.ds(start, 48)], high_buf.at[high], device, 1)
+    send(y_sum.at[pl.ds(pl.multiple_of(64 - half * 64, 64), 80)], cross_buf, across, 1)
     rep_one[...] = repeat_weights(one_ref)
     fill_band(band_one, rep_one)
-    finish(high_buf.at[pl.ds(0, 3)], 1)
-    total = y_sum[pl.ds(pl.multiple_of(high * 32, 32), 48)].astype(F32)
-    for step in range(1, 4):
-        total = total + high_buf[(high + step) % 4].astype(F32)
-    high_sum[...] = total
+    finish(cross_buf, 1)
+    total = y_sum[pl.ds(pl.multiple_of(half * 64, 64), 80)].astype(F32) + cross_buf[...].astype(F32)
+    cross_sum[...] = total.astype(BF16)
+    send(cross_sum.at[pl.ds(pl.multiple_of(32 - odd * 32, 32), 48)], high_buf, beside, 10)
+
+    @pl.when(has_before)
+    def _():
+        finish(cot_buf.at[0], 3)
+
+    @pl.when(jnp.logical_not(has_before))
+    def _():
+        cot_buf[0] = jnp.zeros((128, 256), BF16)
+
+    @pl.when(has_after)
+    def _():
+        finish(cot_buf.at[1], 9)
+
+    @pl.when(jnp.logical_not(has_after))
+    def _():
+        cot_buf[1] = jnp.zeros((128, 256), BF16)
+
+    def cot_before(n):
+        return cot_buf[0, n * 64 : n * 64 + 64].astype(F32).reshape(8, 8, 256)
+
+    def cot_own(n):
+        return cot_ref[n * 64 : n * 64 + 64].astype(F32).reshape(8, 8, 256)
+
+    def cot_after(n):
+        return cot_buf[1, n * 64 : n * 64 + 64].astype(F32).reshape(8, 8, 256)
+
+    fill_windows(win_cot, links_ref, position, cot_before, cot_own, cot_after)
+    finish(high_buf, 10)
+    kept = cross_sum[pl.ds(pl.multiple_of(odd * 32, 32), 48)].astype(F32)
+    high_sum[...] = kept + high_buf[...].astype(F32)
     for step in range(1, 4):
         other, device = near(step)
         start = pl.multiple_of(other * 8, 8)
         send(high_sum.at[pl.ds(start, 24)], low_buf.at[low], device, 2)
 
-    finish(cot_buf, 3)
-
-    def cot_before(n):
-        return cot_buf[0, n * 64 : n * 64 + 64].astype(F32).reshape(8, 8, 256)
-
-    def cot_own(n):
-        return cot_ref[n * 64 : n * 64 + 64].astype(F32).reshape(8, 8, 256)
-
-    def cot_after(n):
-        return cot_buf[1, n * 64 : n * 64 + 64].astype(F32).reshape(8, 8, 256)
-
-    fill_windows(win_cot, links_ref, position, cot_before, cot_own, cot_after)
     back = convolve_back(win_cot, band_back)
     finish(low_buf.at[pl.ds(0, 3)], 2)
 
@@ -380,27 +440,58 @@
     sigmoid = 1.0 / (1.0 + jnp.exp(-pre))
     hidden = (pre * sigmoid).astype(BF16)
     hid_ref[...] = hidden
-    send(hid_ref, hid_buf.at[0], after, 4)
-    send(hid_ref, hid_buf.at[1], before, 4)
     grad_pre = (back * sigmoid * (1.0 + pre * (1.0 - sigmoid))).astype(BF16)
 
-    turned_hidden = jnp.transpose(hidden.astype(F32)).astype(BF16)
-    turned_grad = jnp.transpose(grad_pre.astype(F32)).astype(BF16)
-    weight_products(turned_hidden, win_cot, parts_ref, 14, True)
-    weight_products(turned_grad, win_lift, parts_ref, 0, False)
+    def send_parts(first, last):
+        for part in range(first, last):
+
+            @pl.when(part != me)
+            def _():
+                device = {"space": (part // 8) * 16 + depth, "dp": part % 8}
+                send(parts_ref.at[part], first_buf.at[me], device, 5)
+
     for k in range(28, 32):
         parts_ref[k] = jnp.zeros((16, 128), F32)
-
-    for step in range(1, 32):
-        other, device = wide(step)
-        send(parts_ref.at[other], first_buf.at[me], device, 5)
+    turned_hidden = jnp.transpose(hidden.astype(F32)).astype(BF16)
+    weight_products(turned_hidden, win_cot, parts_ref, 14, True)
+    send_parts(14, 32)
+    turned_grad = jnp.transpose(grad_pre.astype(F32)).astype(BF16)
+    weight_products(turned_grad, win_lift, parts_ref, 0, False)
+    send_parts(0, 14)
+
+    @pl.when(has_after)
+    def _():
+        send(hid_ref, hid_buf.at[0], after, 4)
+
+    @pl.when(has_before)
+    def _():
+        send(hid_ref, hid_buf.at[1], before, 11)
+
     fill_band(band_two, rep_two)
     finish(first_buf.at[pl.ds(0, 31)], 5)
     first_buf[me] = parts_ref[me]
     near_buf[low] = jnp.sum(first_buf[...], axis=0)
     for step in range(1, 4):
         send(near_buf.at[low], near_buf.at[low], near(step)[1], 6)
-    finish(hid_buf, 4)
+    finish(near_buf.at[pl.ds(0, 3)], 6)
+    far_own[0] = (near_buf[0] + near_buf[1]) + (near_buf[2] + near_buf[3])
+    send(far_own.at[0], far_buf.at[0], across, 7)
+
+    @pl.when(has_before)
+    def _():
+        finish(hid_buf.at[0], 4)
+
+    @pl.when(jnp.logical_not(has_before))
+    def _():
+        hid_buf[0] = jnp.zeros((128, 256), BF16)
+
+    @pl.when(has_after)
+    def _():
+        finish(hid_buf.at[1], 11)
+
+    @pl.when(jnp.logical_not(has_after))
+    def _():
+        hid_buf[1] = jnp.zeros((128, 256), BF16)
 
     def hid_of(ref):
         def part(n):
@@ -411,50 +502,67 @@
     fill_windows(
         win_hid, links_ref, position, hid_of(hid_buf.at[0]), hid_of(hid_ref), hid_of(hid_buf.at[1])
     )
-    finish(near_buf.at[pl.ds(0, 3)], 6)
-    far_buf[high] = (near_buf[0] + near_buf[1]) + (near_buf[2] + near_buf[3])
-    for step in range(1, 4):
-        send(far_buf.at[high], far_buf.at[high], far(step)[1], 7)
+    finish(far_buf.at[0], 7)
+    far_own[1] = far_own[0] + far_buf[0]
+    send(far_own.at[1], far_buf.at[1], beside, 12)
     second = convolve(win_hid, band_two)
-    scale = 1.0 / math.sqrt(8 * 128 * 512)
-    finish(far_buf.at[pl.ds(0, 3)], 7)
-    total_ref[me] = ((far_buf[0] + far_buf[1]) + (far_buf[2] + far_buf[3])) * scale
-    for step in range(1, 32):
-        send(total_ref.at[me], total_ref.at[me], wide(step)[1], 8)
     fine = second.reshape(8, 16, 256) + lifted_ref[1]
     for n in range(2):
         fine_ref[n * 64 : n * 64 + 64] = fine[:, n * 8 : n * 8 + 8, :].reshape(64, 256).astype(BF16)
+    scale = 1.0 / math.sqrt(8 * 128 * 512)
+    finish(far_buf.at[1], 12)
+    total_ref[me] = (far_own[1] + far_buf[1]) * scale
+    for step in range(1, 32):
+        send(total_ref.at[me], total_ref.at[me], wide(step)[1], 8)
     finish(total_ref.at[pl.ds(0, 31)], 8)
 
+    sums_ref[...] = total_ref[...]
+
+    sent(y_buf.at[pl.ds(0, 3)], 0)
+    sent(cross_buf, 1)
+    sent(high_buf, 10)
+    sent(low_buf.at[pl.ds(0, 3)], 2)
+
+    @pl.when(has_after)
+    def _():
+        sent(cot_buf.at[0], 3)
+        sent(hid_buf.at[0], 4)
+
+    @pl.when(has_before)
+    def _():
+        sent(cot_buf.at[1], 9)
+        sent(hid_buf.at[1], 11)
+
+    sent(first_buf.at[pl.ds(0, 31)], 5)
+    sent(near_buf.at[pl.ds(0, 3)], 6)
+    sent(far_buf.at[0], 7)
+    sent(far_buf.at[1], 12)
+    sent(total_ref.at[pl.ds(0, 31)], 8)
+
+
+def unpack_kernel(sums_ref, given_ref, fine_ref, grad_one_ref, grad_two_ref):
+    fine_ref[...] = given_ref[...]
     for k in range(7):
-        packed = total_ref[2 * k : 2 * k + 2].reshape(32, 128)
+        packed = sums_ref[2 * k : 2 * k + 2].reshape(32, 128)
         turned = jnp.transpose(packed).reshape(4, 32, 32)
         count = min(4, 27 - 4 * k)
         grad_one_ref[4 * k : 4 * k + count] = turned[0:count]
-        packed = total_ref[14 + 2 * k : 14 + 2 * k + 2].reshape(32, 128)
+        packed = sums_ref[14 + 2 * k : 14 + 2 * k + 2].reshape(32, 128)
         for j in range(count):
             moved = packed if j == 0 else pltpu.roll(packed, 128 - 32 * j, 1)
             grad_two_ref[4 * k + j] = moved[:, 0:32]
 
-    sent(y_buf.at[pl.ds(0, 3)], 0)
-    sent(high_buf.at[pl.ds(0, 3)], 1)
-    sent(low_buf.at[pl.ds(0, 3)], 2)
-    sent(cot_buf, 3)
-    sent(hid_buf, 4)
-    sent(first_buf.at[pl.ds(0, 31)], 5)
-    sent(near_buf.at[pl.ds(0, 3)], 6)
-    sent(far_buf.at[pl.ds(0, 3)], 7)
-    sent(total_ref.at[pl.ds(0, 31)], 8)
-
 
 def body(coarse_latents, active_blocks, face_links, cotangent, up_weight, conv_one, conv_two):
     vmem = pl.BlockSpec(memory_space=pltpu.VMEM)
-    smem = pl.BlockSpec(memory_space=pltpu.SMEM)
+    outside = pl.BlockSpec(memory_space=pl.ANY)
     scratch = [
         ((528, 128), BF16),
         ((4, 144, 128), BF16),
         ((144, 128), BF16),
-        ((4, 48, 128), BF16),
+        ((80, 128), BF16),
+        ((80, 128), BF16),
+        ((48, 128), BF16),
         ((48, 128), F32),
         ((4, 24, 128), F32),
         ((2, 128, 256), BF16),
@@ -473,22 +581,33 @@
         ((32, 16, 128), F32),
         ((32, 16, 128), F32),
         ((4, 16, 128), F32),
-        ((4, 16, 128), F32),
+        ((2, 16, 128), F32),
+        ((2, 16, 128), F32),
         ((32, 16, 128), F32),
     ]
-    fine, grad_one, grad_two = pl.pallas_call(
+    inputs = [
+        pltpu.VMEM((64, 512), BF16),
+        pltpu.VMEM((1, 128), jnp.int32),
+        pltpu.SMEM((2, 6), jnp.int32),
+        pltpu.VMEM((128, 256), BF16),
+        pltpu.VMEM((64, 2048), BF16),
+        pltpu.VMEM((864, 32), BF16),
+        pltpu.VMEM((864, 32), BF16),
+    ]
+    out_shape = (
+        jax.ShapeDtypeStruct((128, 256), BF16),
+        jax.ShapeDtypeStruct((32, 16, 128), F32),
+    )
+    given, sums = pl.pallas_call(
         step_kernel,
-        out_shape=(
-            jax.ShapeDtypeStruct((128, 256), BF16),
-            jax.ShapeDtypeStruct((27, 32, 32), F32),
-            jax.ShapeDtypeStruct((27, 32, 32), F32),
-        ),
-        in_specs=[vmem, vmem, smem, vmem, vmem, vmem, vmem],
-        out_specs=(vmem, vmem, vmem),
-        scratch_shapes=[pltpu.VMEM(*one) for one in scratch]
-        + [pltpu.SemaphoreType.DMA((9,)), pltpu.SemaphoreType.DMA((9,))],
+        out_shape=out_shape,
+        in_specs=[outside] * 7,
+        out_specs=(vmem, vmem),
+        scratch_shapes=inputs
+        + [pltpu.VMEM(*one) for one in scratch]
+        + [pltpu.SemaphoreType.DMA((count,)) for count in (13, 13, 7)],
         compiler_params=pltpu.CompilerParams(
-            collective_id=0, has_side_effects=True, vmem_limit_bytes=40 * 1024 * 1024
+            collective_id=0, has_side_effects=True, vmem_limit_bytes=62 * 1024 * 1024
         ),
     )(
         coarse_latents[0],
@@ -499,6 +618,16 @@
         conv_one.reshape(864, 32),
         conv_two.reshape(864, 32),
     )
+    fine, grad_one, grad_two = pl.pallas_call(
+        unpack_kernel,
+        out_shape=(
+            jax.ShapeDtypeStruct((128, 256), BF16),
+            jax.ShapeDtypeStruct((27, 32, 32), F32),
+            jax.ShapeDtypeStruct((27, 32, 32), F32),
+        ),
+        in_specs=[vmem] * 2,
+        out_specs=(vmem,) * 3,
+    )(sums, given)
     return fine.reshape(1, 2, 8, 8, 256), grad_one, grad_two
 
 

time: 66.4 us -> 61.4 us (0.925)
  local copies, waits for them, and re-layouts: 7.32 us -> 0 us
  Pallas kernels: 58.1 us -> 60.6 us
    unnamed x17 -> x0, local copies, waits for them, and re-layouts: 7.32 us -> none
    pallas_call x1 -> x2, Pallas kernels: 58.1 us -> 60.6 us  [the longest x1 58.5 us: body(): pl.pallas_call(step_kernel, out_shape=out_shape, in_specs=[outside] * 7,...]
where the time goes in v2:
time: 61.4 us; the launch traced here: 61.2 us
  Pallas kernels  60.6 us (99%)
  between operations  0.64 us (1%)
    pallas_call x1, Pallas kernels, body(): pl.pallas_call(step_kernel, out_shape=out_shape, in_specs=[outside] * 7,...  58.5 us
    pallas_call x1, Pallas kernels, body(): pl.pallas_call(unpack_kernel, out_shape=(jax.ShapeDtypeStruct((128, 256),...  2.08 us

profile of v2, /device:TPU:1, one launch (start us, length us, event | category | flops | bytes accessed | tf_op | source)
XLA Modules:
  0.0 61.2 jit_solution(15025300961471265310)
XLA Ops:
  0.6 58.5 %shard_map.94 = (bf16[128,256]{1,0:T(8,128)(2,1)}, f32[32,16,128]{2,1,0:T(8,128)}) custom-call(bf16[64,512]{1,0:T(8,128)(2,1)} %bitcast.8, s32[1,128]{1,0:T(1,128)} %active_in.1, s32[2,6]{1,0:T(2,128)} %bitcast.10, bf16[128,256]{1,0:T(8,128)(2,1)} %bitcast.9, bf16[64,2048]{1,0:T(8,128)(2,1)} %up_in.1, bf16[864,32]{1,0:T(8,128)(2,1)} %bitcast.6, ...), custom_call_target="tpu_custom_call" | custom-call | tf_op jit(solution)/shard_map/pallas_call | solution.py:601
  59.1 2.1 %shard_map.95 = (bf16[128,256]{1,0:T(8,128)(2,1)}, f32[27,32,32]{2,1,0:T(8,128)}, f32[27,32,32]{2,1,0:T(8,128)}) custom-call(f32[32,16,128]{2,1,0:T(8,128)} %get-tuple-element.8.sums_ref, bf16[128,256]{1,0:T(8,128)(2,1)} %get-tuple-element.9.given_ref), custom_call_target="tpu_custom_call" | custom-call | tf_op jit(solution)/shard_map/pallas_call | solution.py:621

commit v3 on v2

--- a/solution.py
+++ b/solution.py
@@ -252,12 +252,12 @@
     parts_ref,
     first_buf,
     near_buf,
-    far_own,
     far_buf,
     total_ref,
     send_sems,
     recv_sems,
     copy_sems,
+    ready_sem,
 ):
     position = lax.axis_index("space")
     dp = lax.axis_index("dp")
@@ -265,9 +265,13 @@
     low, high = depth % 4, depth // 4
     me = row * 8 + dp
 
-    def wide(step):
-        other = (me + step) % 32
-        return other, {"space": (other // 8) * 16 + depth, "dp": other % 8}
+    def farthest_first():
+        for dy in (2, 1, 3, 0):
+            for dx in (2, 1, 3, 0):
+                for flip in (1, 0):
+                    if dy or dx or flip:
+                        column = ((dp // 2 + dx) % 4) * 2 + (dp + flip) % 2
+                        yield {"space": ((row + dy) % 4) * 16 + depth, "dp": column}
 
     def along_y(step):
         other = (row + step) % 4
@@ -283,6 +287,7 @@
     half, odd = high // 2, high % 2
     across = far(3 - high)
     beside = far(high + 1 - 2 * odd)
+    opposite = far((high + 2) % 4)
     after = {"space": position + 1, "dp": dp}
     before = {"space": position - 1, "dp": dp}
     has_after, has_before = position < 63, position > 0
@@ -304,8 +309,8 @@
 
     for step in range(1, 4):
         greet(near(step)[1])
-    for step in range(1, 32):
-        greet(wide(step)[1])
+    for device in farthest_first():
+        greet(device)
 
     sources = (coarse_in, active_in, cot_in, links_in, two_in, up_in, one_in)
     targets = (coarse_ref, active_ref, cot_ref, links_ref, two_ref, up_ref, one_ref)
@@ -397,6 +402,7 @@
 
     fill_windows(win_cot, links_ref, position, cot_before, cot_own, cot_after)
     finish(high_buf, 10)
+    pl.semaphore_signal(ready_sem, inc=1, device_id=opposite, device_id_type=MESH_ID)
     kept = cross_sum[pl.ds(pl.multiple_of(odd * 32, 32), 48)].astype(F32)
     high_sum[...] = kept + high_buf[...].astype(F32)
     for step in range(1, 4):
@@ -474,8 +480,10 @@
     for step in range(1, 4):
         send(near_buf.at[low], near_buf.at[low], near(step)[1], 6)
     finish(near_buf.at[pl.ds(0, 3)], 6)
-    far_own[0] = (near_buf[0] + near_buf[1]) + (near_buf[2] + near_buf[3])
-    send(far_own.at[0], far_buf.at[0], across, 7)
+    far_buf[high] = (near_buf[0] + near_buf[1]) + (near_buf[2] + near_buf[3])
+    pl.semaphore_wait(ready_sem, 1)
+    for device in (opposite, across, beside):
+        send(far_buf.at[high], far_buf.at[high], device, 7)
 
     @pl.when(has_before)
     def _():
@@ -502,18 +510,15 @@
     fill_windows(
         win_hid, links_ref, position, hid_of(hid_buf.at[0]), hid_of(hid_ref), hid_of(hid_buf.at[1])
     )
-    finish(far_buf.at[0], 7)
-    far_own[1] = far_own[0] + far_buf[0]
-    send(far_own.at[1], far_buf.at[1], beside, 12)
     second = convolve(win_hid, band_two)
     fine = second.reshape(8, 16, 256) + lifted_ref[1]
     for n in range(2):
         fine_ref[n * 64 : n * 64 + 64] = fine[:, n * 8 : n * 8 + 8, :].reshape(64, 256).astype(BF16)
     scale = 1.0 / math.sqrt(8 * 128 * 512)
-    finish(far_buf.at[1], 12)
-    total_ref[me] = (far_own[1] + far_buf[1]) * scale
-    for step in range(1, 32):
-        send(total_ref.at[me], total_ref.at[me], wide(step)[1], 8)
+    finish(far_buf.at[pl.ds(0, 3)], 7)
+    total_ref[me] = ((far_buf[0] + far_buf[1]) + (far_buf[2] + far_buf[3])) * scale
+    for device in farthest_first():
+        send(total_ref.at[me], total_ref.at[me], device, 8)
     finish(total_ref.at[pl.ds(0, 31)], 8)
 
     sums_ref[...] = total_ref[...]
@@ -535,8 +540,7 @@
 
     sent(first_buf.at[pl.ds(0, 31)], 5)
     sent(near_buf.at[pl.ds(0, 3)], 6)
-    sent(far_buf.at[0], 7)
-    sent(far_buf.at[1], 12)
+    sent(far_buf.at[pl.ds(0, 3)], 7)
     sent(total_ref.at[pl.ds(0, 31)], 8)
 
 
@@ -581,8 +585,7 @@
         ((32, 16, 128), F32),
         ((32, 16, 128), F32),
         ((4, 16, 128), F32),
-        ((2, 16, 128), F32),
-        ((2, 16, 128), F32),
+        ((4, 16, 128), F32),
         ((32, 16, 128), F32),
     ]
     inputs = [
@@ -605,7 +608,8 @@
         out_specs=(vmem, vmem),
         scratch_shapes=inputs
         + [pltpu.VMEM(*one) for one in scratch]
-        + [pltpu.SemaphoreType.DMA((count,)) for count in (13, 13, 7)],
+        + [pltpu.SemaphoreType.DMA((count,)) for count in (13, 13, 7)]
+        + [pltpu.SemaphoreType.REGULAR],
         compiler_params=pltpu.CompilerParams(
             collective_id=0, has_side_effects=True, vmem_limit_bytes=62 * 1024 * 1024
         ),

time: 61.4 us -> 59.4 us (0.967)
  Pallas kernels: 60.6 us -> 58.6 us
    pallas_call x1, Pallas kernels: 58.5 us -> 56.5 us  [body(): pl.pallas_call(step_kernel, out_shape=out_shape, in_specs=[outside] * 7,...]
where the time goes in v3:
time: 59.4 us; the launch traced here: 59.3 us
  Pallas kernels  58.6 us (99%)
  between operations  0.64 us (1%)
    pallas_call x1, Pallas kernels, body(): pl.pallas_call(step_kernel, out_shape=out_shape, in_specs=[outside] * 7,...  56.5 us
    pallas_call x1, Pallas kernels, body(): pl.pallas_call(unpack_kernel, out_shape=(jax.ShapeDtypeStruct((128, 256),...  2.08 us

profile of v3, /device:TPU:1, one launch (start us, length us, event | category | flops | bytes accessed | tf_op | source)
XLA Modules:
  0.0 59.3 jit_solution(3317181496621600232)
XLA Ops:
  0.6 56.5 %shard_map.94 = (bf16[128,256]{1,0:T(8,128)(2,1)}, f32[32,16,128]{2,1,0:T(8,128)}) custom-call(bf16[64,512]{1,0:T(8,128)(2,1)} %bitcast.8, s32[1,128]{1,0:T(1,128)} %active_in.1, s32[2,6]{1,0:T(2,128)} %bitcast.10, bf16[128,256]{1,0:T(8,128)(2,1)} %bitcast.9, bf16[64,2048]{1,0:T(8,128)(2,1)} %up_in.1, bf16[864,32]{1,0:T(8,128)(2,1)} %bitcast.6, ...), custom_call_target="tpu_custom_call" | custom-call | tf_op jit(solution)/shard_map/pallas_call | solution.py:604
  57.2 2.1 %shard_map.95 = (bf16[128,256]{1,0:T(8,128)(2,1)}, f32[27,32,32]{2,1,0:T(8,128)}, f32[27,32,32]{2,1,0:T(8,128)}) custom-call(f32[32,16,128]{2,1,0:T(8,128)} %get-tuple-element.8.sums_ref, bf16[128,256]{1,0:T(8,128)(2,1)} %get-tuple-element.9.given_ref), custom_call_target="tpu_custom_call" | custom-call | tf_op jit(solution)/shard_map/pallas_call | solution.py:625

commit v4 on v3

--- a/solution.py
+++ b/solution.py
@@ -219,7 +219,7 @@
     up_in,
     one_in,
     two_in,
-    fine_ref,
+    fine_out,
     sums_ref,
     coarse_ref,
     active_ref,
@@ -258,6 +258,7 @@
     recv_sems,
     copy_sems,
     ready_sem,
+    fine_ref,
 ):
     position = lax.axis_index("space")
     dp = lax.axis_index("dp")
@@ -514,6 +515,8 @@
     fine = second.reshape(8, 16, 256) + lifted_ref[1]
     for n in range(2):
         fine_ref[n * 64 : n * 64 + 64] = fine[:, n * 8 : n * 8 + 8, :].reshape(64, 256).astype(BF16)
+    fine_copy = pltpu.make_async_copy(fine_ref, fine_out, copy_sems.at[7])
+    fine_copy.start()
     scale = 1.0 / math.sqrt(8 * 128 * 512)
     finish(far_buf.at[pl.ds(0, 3)], 7)
     total_ref[me] = ((far_buf[0] + far_buf[1]) + (far_buf[2] + far_buf[3])) * scale
@@ -522,6 +525,7 @@
     finish(total_ref.at[pl.ds(0, 31)], 8)
 
     sums_ref[...] = total_ref[...]
+    fine_copy.wait()
 
     sent(y_buf.at[pl.ds(0, 3)], 0)
     sent(cross_buf, 1)
@@ -544,8 +548,9 @@
     sent(total_ref.at[pl.ds(0, 31)], 8)
 
 
-def unpack_kernel(sums_ref, given_ref, fine_ref, grad_one_ref, grad_two_ref):
-    fine_ref[...] = given_ref[...]
+def unpack_kernel(sums_ref, given_ref, fine_ref, grad_one_ref, grad_two_ref, sem):
+    fine_copy = pltpu.make_async_copy(given_ref, fine_ref, sem)
+    fine_copy.start()
     for k in range(7):
         packed = sums_ref[2 * k : 2 * k + 2].reshape(32, 128)
         turned = jnp.transpose(packed).reshape(4, 32, 32)
@@ -555,6 +560,7 @@
         for j in range(count):
             moved = packed if j == 0 else pltpu.roll(packed, 128 - 32 * j, 1)
             grad_two_ref[4 * k + j] = moved[:, 0:32]
+    fine_copy.wait()
 
 
 def body(coarse_latents, active_blocks, face_links, cotangent, up_weight, conv_one, conv_two):
@@ -605,11 +611,11 @@
         step_kernel,
         out_shape=out_shape,
         in_specs=[outside] * 7,
-        out_specs=(vmem, vmem),
+        out_specs=(outside, vmem),
         scratch_shapes=inputs
         + [pltpu.VMEM(*one) for one in scratch]
-        + [pltpu.SemaphoreType.DMA((count,)) for count in (13, 13, 7)]
-        + [pltpu.SemaphoreType.REGULAR],
+        + [pltpu.SemaphoreType.DMA((count,)) for count in (13, 13, 8)]
+        + [pltpu.SemaphoreType.REGULAR, pltpu.VMEM((128, 256), BF16)],
         compiler_params=pltpu.CompilerParams(
             collective_id=0, has_side_effects=True, vmem_limit_bytes=62 * 1024 * 1024
         ),
@@ -629,8 +635,9 @@
             jax.ShapeDtypeStruct((27, 32, 32), F32),
             jax.ShapeDtypeStruct((27, 32, 32), F32),
         ),
-        in_specs=[vmem] * 2,
-        out_specs=(vmem,) * 3,
+        in_specs=[vmem, outside],
+        out_specs=(outside, vmem, vmem),
+        scratch_shapes=[pltpu.SemaphoreType.DMA(())],
     )(sums, given)
     return fine.reshape(1, 2, 8, 8, 256), grad_one, grad_two
 

time: 59.4 us -> 62.3 us (1.049)
  Pallas kernels: 58.6 us -> 61.5 us
    pallas_call x1, Pallas kernels: 2.08 us -> 4.95 us  [body(): pl.pallas_call(unpack_kernel, out_shape=(jax.ShapeDtypeStruct((128, 256),...]
where the time goes in v4:
time: 62.3 us; the launch traced here: 62.1 us
  Pallas kernels  61.5 us (99%)
  between operations  0.64 us (1%)
    pallas_call x1, Pallas kernels, body(): pl.pallas_call(step_kernel, out_shape=out_shape, in_specs=[outside] * 7,...  56.5 us
    pallas_call x1, Pallas kernels, body(): pl.pallas_call(unpack_kernel, out_shape=(jax.ShapeDtypeStruct((128, 256),...  4.95 us

profile of v4, /device:TPU:1, one launch (start us, length us, event | category | flops | bytes accessed | tf_op | source)
XLA Modules:
  0.0 62.1 jit_solution(4712427672107718793)
XLA Ops:
  0.6 56.5 %shard_map.94 = (bf16[128,256]{1,0:T(8,128)(2,1)}, f32[32,16,128]{2,1,0:T(8,128)}) custom-call(bf16[64,512]{1,0:T(8,128)(2,1)} %bitcast.8, s32[1,128]{1,0:T(1,128)} %active_in.1, s32[2,6]{1,0:T(2,128)} %bitcast.10, bf16[128,256]{1,0:T(8,128)(2,1)} %bitcast.9, bf16[64,2048]{1,0:T(8,128)(2,1)} %up_in.1, bf16[864,32]{1,0:T(8,128)(2,1)} %bitcast.6, ...), custom_call_target="tpu_custom_call" | custom-call | tf_op jit(solution)/shard_map/pallas_call | solution.py:610
  57.2 5.0 %shard_map.95 = (bf16[128,256]{1,0:T(8,128)(2,1)}, f32[27,32,32]{2,1,0:T(8,128)}, f32[27,32,32]{2,1,0:T(8,128)}) custom-call(f32[32,16,128]{2,1,0:T(8,128)} %get-tuple-element.8.sums_ref, bf16[128,256]{1,0:T(8,128)(2,1)} %get-tuple-element.9.given_ref), custom_call_target="tpu_custom_call" | custom-call | tf_op jit(solution)/shard_map/pallas_call | solution.py:631

commit v5 on v3

--- a/solution.py
+++ b/solution.py
@@ -464,21 +464,21 @@
     turned_grad = jnp.transpose(grad_pre.astype(F32)).astype(BF16)
     weight_products(turned_grad, win_lift, parts_ref, 0, False)
     send_parts(0, 14)
-
-    @pl.when(has_after)
-    def _():
-        send(hid_ref, hid_buf.at[0], after, 4)
-
-    @pl.when(has_before)
-    def _():
-        send(hid_ref, hid_buf.at[1], before, 11)
-
     fill_band(band_two, rep_two)
     finish(first_buf.at[pl.ds(0, 31)], 5)
     first_buf[me] = parts_ref[me]
     near_buf[low] = jnp.sum(first_buf[...], axis=0)
     for step in range(1, 4):
         send(near_buf.at[low], near_buf.at[low], near(step)[1], 6)
+
+    @pl.when(has_after)
+    def _():
+        send(hid_ref, hid_buf.at[0], after, 4)
+
+    @pl.when(has_before)
+    def _():
+        send(hid_ref, hid_buf.at[1], before, 11)
+
     finish(near_buf.at[pl.ds(0, 3)], 6)
     far_buf[high] = (near_buf[0] + near_buf[1]) + (near_buf[2] + near_buf[3])
     pl.semaphore_wait(ready_sem, 1)

time: 59.4 us -> 59 us (level)
  no operation moved by 1% of the time
where the time goes in v5:
time: 59 us; the launch traced here: 58.9 us
  Pallas kernels  58.2 us (99%)
  between operations  0.64 us (1%)
    pallas_call x1, Pallas kernels, body(): pl.pallas_call(step_kernel, out_shape=out_shape, in_specs=[outside] * 7,...  56.1 us
    pallas_call x1, Pallas kernels, body(): pl.pallas_call(unpack_kernel, out_shape=(jax.ShapeDtypeStruct((128, 256),...  2.08 us

profile of v5, /device:TPU:1, one launch (start us, length us, event | category | flops | bytes accessed | tf_op | source)
XLA Modules:
  0.0 58.9 jit_solution(13885672176047397813)
XLA Ops:
  0.6 56.1 %shard_map.94 = (bf16[128,256]{1,0:T(8,128)(2,1)}, f32[32,16,128]{2,1,0:T(8,128)}) custom-call(bf16[64,512]{1,0:T(8,128)(2,1)} %bitcast.8, s32[1,128]{1,0:T(1,128)} %active_in.1, s32[2,6]{1,0:T(2,128)} %bitcast.10, bf16[128,256]{1,0:T(8,128)(2,1)} %bitcast.9, bf16[64,2048]{1,0:T(8,128)(2,1)} %up_in.1, bf16[864,32]{1,0:T(8,128)(2,1)} %bitcast.6, ...), custom_call_target="tpu_custom_call" | custom-call | tf_op jit(solution)/shard_map/pallas_call | solution.py:604
  56.8 2.1 %shard_map.95 = (bf16[128,256]{1,0:T(8,128)(2,1)}, f32[27,32,32]{2,1,0:T(8,128)}, f32[27,32,32]{2,1,0:T(8,128)}) custom-call(f32[32,16,128]{2,1,0:T(8,128)} %get-tuple-element.8.sums_ref, bf16[128,256]{1,0:T(8,128)(2,1)} %get-tuple-element.9.given_ref), custom_call_target="tpu_custom_call" | custom-call | tf_op jit(solution)/shard_map/pallas_call | solution.py:625
